TPU v7x, 32 devices: a whole 2x2x4 slice. The times are simulated.
32 devices in a mesh: neuron: 4 (over x, core), box: 4 (over z), spec: 2 (over y).
Axes of the slice: x: 2, y: 2, z: 4, core: 2. Of those that a mesh axis runs over, the one named last changes fastest.
Arguments:
- coeff: bfloat16 [96, 8, 8192], P('box', 'spec', 'neuron'), may hold values from -6 to 6
- weight: bfloat16 [8192, 8192], P('neuron', 'spec'), may hold values from -0.09375 to 0.09375
- upper_bound: float32 [96, 8192], P('box', 'neuron'), may hold values from 0.2 to 6, as said below
- lower_depth: float32 [96, 8192], P('box', 'neuron'), may hold values from 0.2 to 6, as said below
- slopes: float32 [96, 8192], P('box', 'neuron'), may hold values from 0 to 1
- state: int32 [96, 8192], P('box', 'neuron'), may hold values from 0 to 2
- adjoint: bfloat16 [96, 8, 8192], P('box', 'spec', 'neuron'), may hold values from -6 to 6
Outputs:
- new_coeff: bfloat16 [96, 8, 8192], P('box', 'spec', 'neuron')
- offset: float32 [96, 8], P('box', 'spec')
- slope_grad: float32 [96, 8192], P('box', 'neuron')
- coeff_grad: bfloat16 [96, 8, 8192], P('box', 'spec', 'neuron')
Inputs may be any that keep to these rules, and one draw needn't show every extreme that they name: `upper_bound`: positive. `lower_depth`: positive.
All inputs are finite; a program needn't handle non-finite values.
Results may differ from a plain program's by a relative error of at most 0.0095.
Values may be sent and summed in bfloat16 or wider, within the bound.
A program may use at most 64 MiB of HBM per device.

v0:
```python
import functools

import jax
import jax.numpy as jnp
from jax import lax
from jax.experimental import pallas as pl
from jax.experimental.pallas import tpu as pltpu
from jax.sharding import PartitionSpec as P

MESH = pl.DeviceIdType.MESH
F32 = jnp.float32
BF16 = jnp.bfloat16


def kernel(
    n, boxes, specs, tile, scale,
    coeff, weight, upper_in, depth_in, slopes_in, state_in, adjoint,
    new_coeff, offset, slope_grad, coeff_grad,
    upper, depth, slopes, state, held, other, mine, theirs, crossed, parts, params, t_params, t_adjoint, cotan,
    nc_out, nc_in, sg_out, sg_in, kept, away, back, off_part, offs,
    i_sem, w_sem, a_sem, t_send, t_recv, c_send, c_recv, b_send, b_recv, g_send, g_recv, f_send,
    n_sem, s_send, s_recv, e_send, e_recv, o_send, o_recv,
):
    me, sp = lax.axis_index("neuron"), lax.axis_index("spec")
    h = n // 2
    per_core = h // 2
    core, chip = lax.rem(me, 2), lax.div(me, 2)
    mate = me + 1 - 2 * core
    half = 1 - lax.div(me, h)
    home = sp * h + lax.rem(me, h)
    owner, owner_spec = (1 - sp) * h + lax.rem(me, h), lax.div(me, h)
    rows, width = coeff.shape
    tiles = width // tile

    def remote(src, dst, send, recv, neuron, spec):
        return pltpu.make_async_remote_copy(
            src_ref=src, dst_ref=dst, send_sem=send, recv_sem=recv,
            device_id={"neuron": neuron, "spec": spec}, device_id_type=MESH,
        )

    def order(k):
        j = lax.rem(k, per_core)
        return 2 * j + jnp.where(k < per_core, 1 - core, core)

    def columns(q, t):
        return pl.ds(pl.multiple_of(q * width + t * tile, tile), tile)

    def load(k):
        q, t = order(lax.div(k, tiles)), lax.rem(k, tiles)
        return pltpu.make_async_copy(
            weight.at[:, columns(q, t)], held.at[:, columns(q, t)], w_sem.at[k]
        )

    bounds = [
        pltpu.make_async_copy(src, dst, i_sem.at[k])
        for k, (src, dst) in enumerate(
            ((upper_in, upper), (depth_in, depth), (slopes_in, slopes), (state_in, state))
        )
    ]
    for copy in bounds:
        copy.start()

    @pl.loop(0, h * tiles)
    def _(k):
        load(k).start()

    barrier = pltpu.get_barrier_semaphore()
    for d in range(1, 2 * n):
        flat = lax.rem(me * 2 + sp + d, 2 * n)
        pl.semaphore_signal(
            barrier, inc=1,
            device_id={"neuron": lax.div(flat, 2), "spec": lax.rem(flat, 2)},
            device_id_type=MESH,
        )

    pl.semaphore_wait(barrier, 2 * n - 1)

    a_copy = remote(coeff, other, a_sem.at[0], a_sem.at[1], me, 1 - sp)
    a_copy.start()
    adjoint_copy = remote(adjoint, t_adjoint, t_send.at[0], t_recv.at[0], owner, owner_spec)
    adjoint_copy.start()
    for copy in bounds:
        copy.wait()
    up = upper[...]
    unstable = state[...] == 2
    solid = jnp.where(state[...] == 1, 1.0, 0.0)
    params[...] = jnp.concatenate(
        [
            jnp.where(unstable, slopes[...], solid),
            jnp.where(unstable, up / (up + depth[...]), solid),
        ],
        axis=0,
    ).astype(BF16)
    params_copy = remote(params, t_params, t_send.at[1], t_recv.at[1], owner, owner_spec)
    params_copy.start()

    def core_copy(st, j, t):
        cols = columns(0, t)
        return remote(
            theirs.at[st, j, :, cols], crossed.at[st, j, :, cols],
            c_send.at[st, j, t], c_recv.at[st, j, t], mate, sp,
        )

    def part_copy(st, j, t):
        spec_half = sp if st == 0 else 1 - sp
        target = (1 - spec_half) * per_core + j
        cols = columns(0, t)
        return target, remote(
            mine.at[st, j, :, cols], parts.at[chip, :, cols],
            b_send.at[st, j, t], b_recv.at[chip, t], target * 2 + core, sp,
        )

    for st in range(2):
        if st == 1:
            a_copy.wait()
        rows_in = coeff if st == 0 else other

        @pl.loop(0, per_core * tiles)
        def _(k):
            j, t = lax.div(k, tiles), lax.rem(k, tiles)
            if st == 0:
                load(k).wait()
            theirs[st, j, :, columns(0, t)] = jnp.dot(
                rows_in[...], held[:, columns(2 * j + 1 - core, t)], preferred_element_type=F32
            )
            core_copy(st, j, t).start()

        @pl.loop(0, per_core * tiles)
        def _(k):
            j, t = lax.div(k, tiles), lax.rem(k, tiles)
            cols = columns(0, t)
            if st == 0:
                load(k + per_core * tiles).wait()
            total = jnp.dot(
                rows_in[...], held[:, columns(2 * j + core, t)], preferred_element_type=F32
            )
            core_copy(st, j, t).wait()
            mine[st, j, :, cols] = total + crossed[st, j, :, cols]
            target, copy = part_copy(st, j, t)

            @pl.when(target != chip)
            def _():
                copy.start()

    own_stage = jnp.where(half == sp, 0, 1)
    own_j = lax.rem(chip, per_core)
    adjoint_copy.wait()
    params_copy.wait()

    def g_copy(p, t):
        cols = columns(0, t)
        return remote(
            cotan.at[me, :, cols], cotan.at[me, :, cols],
            g_send.at[p, t], g_recv.at[me, t], p * 2 + core, sp,
        )

    def own_core_copy(t):
        cols = columns(0, t)
        return remote(
            cotan.at[me, :, cols], cotan.at[me, :, cols],
            g_send.at[chip, t], g_recv.at[me, t], mate, sp,
        )

    @pl.loop(0, tiles)
    def _(t):
        cols = columns(0, t)
        pre = mine[own_stage, own_j, :, cols]
        for d in range(1, h):
            source = lax.rem(chip + d, h)
            pltpu.make_async_remote_copy(
                src_ref=mine.at[0, 0, :, cols], dst_ref=parts.at[source, :, cols],
                send_sem=b_send.at[0, 0, t], recv_sem=b_recv.at[source, t],
                device_id={"neuron": mate, "spec": sp}, device_id_type=MESH,
            ).wait_recv()
            pre = pre + parts[source, :, cols]
        both = t_params[:, cols].astype(F32)
        low = jnp.concatenate([both[:boxes]] * specs, axis=0)
        high = jnp.concatenate([both[boxes:]] * specs, axis=0)
        cot = t_adjoint[:, cols].astype(F32)
        positive = jnp.maximum(pre, 0.0)
        cotan[me, :, cols] = (cot * jnp.where(pre > 0.0, low, high)).astype(BF16)
        nc_out[:, cols] = (low * positive + high * jnp.minimum(pre, 0.0)).astype(BF16)
        terms = cot * positive
        total = terms[:boxes]
        for s in range(1, specs):
            total = total + terms[s * boxes : (s + 1) * boxes]
        sg_out[:, cols] = jnp.concatenate(
            [total, jnp.zeros((sg_out.shape[0] - boxes, tile), F32)], axis=0
        ).astype(BF16)

        for d in range(1, h):
            g_copy(lax.rem(chip + d, h), t).start()
        own_core_copy(t).start()

    nc_copy = remote(nc_out, nc_in, n_sem.at[0], n_sem.at[1], home, half)
    nc_copy.start()
    sg_copy = remote(sg_out, sg_in.at[half], s_send.at[0], s_recv.at[half], home, half)
    sg_copy.start()
    sg_far = remote(sg_out, sg_in.at[half], s_send.at[1], s_recv.at[half], home, 1 - half)
    sg_near = pltpu.make_async_copy(sg_out, sg_in.at[half], s_recv.at[half])
    fixed = home == me

    @pl.when(fixed)
    def _():
        sg_near.start()

    @pl.when(jnp.logical_not(fixed))
    def _():
        sg_far.start()

    def arrival(i, t):
        cols = columns(0, t)
        return pltpu.make_async_remote_copy(
            src_ref=cotan.at[i, :, cols], dst_ref=cotan.at[i, :, cols], send_sem=f_send.at[0, t],
            recv_sem=g_recv.at[i, t], device_id={"neuron": mate, "spec": sp},
            device_id_type=MESH,
        )

    def forward(p, t):
        i = p * 2 + core
        cols = columns(0, t)
        return remote(
            cotan.at[i, :, cols], cotan.at[i, :, cols], f_send.at[p, t], g_recv.at[i, t], mate, sp
        )

    def e_copy(t):
        return remote(
            away.at[:, columns(0, t)], back.at[:, columns(0, t)], e_send.at[t], e_recv.at[t],
            me, 1 - sp,
        )

    def backward(spec_half):
        @pl.loop(0, tiles)
        def _(t):
            line = pl.ds(pl.multiple_of(t * tile, tile), tile)
            total = jnp.zeros((rows, tile), F32)
            for q in range(h):
                total = total + lax.dot_general(
                    cotan[(1 - spec_half) * h + q], held[line, q * width : (q + 1) * width],
                    (((1,), (1,)), ((), ())), preferred_element_type=F32,
                )

            @pl.when(spec_half == sp)
            def _():
                kept[:, columns(0, t)] = total

            @pl.when(spec_half != sp)
            def _():
                away[:, columns(0, t)] = total.astype(BF16)
                e_copy(t).start()

    for spec_half, skip in ((half, True), (1 - half, False)):
        first = (1 - spec_half) * per_core
        for j in range(per_core):
            p = first + j

            def take(p=p):
                @pl.loop(0, tiles)
                def _(t):
                    arrival(p * 2 + core, t).wait_recv()
                    forward(p, t).start()

            if skip:
                pl.when(p != chip)(take)
            else:
                take()

        @pl.loop(0, per_core * tiles)
        def _(k):
            p = first + lax.div(k, tiles)
            arrival(p * 2 + 1 - core, lax.rem(k, tiles)).wait_recv()

        backward(spec_half)

    nc_copy.wait()
    off_part[...] = jnp.zeros_like(off_part)

    @pl.loop(0, tiles)
    def _(t):
        cols = columns(0, t)
        value = nc_in[:, cols]
        new_coeff[:, cols] = value
        bound = jnp.where(state[:, cols] == 2, depth[:, cols], 0.0) * scale
        terms = jnp.minimum(value.astype(F32), 0.0) * jnp.concatenate([bound] * specs, axis=0)
        total = terms[:, :128]
        for c in range(1, tile // 128):
            total = total + terms[:, c * 128 : (c + 1) * 128]
        off_part[:rows, :] += total

    offs[me] = lax.dot_general(
        jnp.ones((8, 128), F32), off_part[...], (((1,), (1,)), ((), ())),
        precision=lax.Precision.HIGHEST, preferred_element_type=F32,
    )

    def o_copy(i):
        return remote(offs.at[me], offs.at[me], o_send.at[i], o_recv.at[me], i, sp)

    for d in range(1, n):
        o_copy(lax.rem(me + d, n)).start()

    def sg_arrival(k):
        return pltpu.make_async_remote_copy(
            src_ref=sg_out, dst_ref=sg_in.at[k], send_sem=s_send.at[1],
            recv_sem=s_recv.at[k], device_id={"neuron": mate, "spec": sp}, device_id_type=MESH,
        )

    sg_copy.wait_send()

    @pl.when(jnp.logical_not(fixed))
    def _():
        sg_far.wait_send()

    for k in range(2):
        sg_arrival(k).wait_recv()
    both = sg_in[0].astype(F32)[:boxes] + sg_in[1].astype(F32)[:boxes]
    slope_grad[...] = jnp.where(state[...] == 2, both, 0.0)

    for t in range(tiles):
        e_copy(t).wait()
        cols = columns(0, t)
        coeff_grad[:, cols] = (kept[:, cols] + back[:, cols].astype(F32)).astype(BF16)

    for d in range(1, n):
        i = lax.rem(me + d, n)
        pltpu.make_async_remote_copy(
            src_ref=offs.at[i], dst_ref=offs.at[i], send_sem=o_send.at[me],
            recv_sem=o_recv.at[i], device_id={"neuron": mate, "spec": sp}, device_id_type=MESH,
        ).wait_recv()
    result = offs[0]
    for i in range(1, n):
        result = result + offs[i]
    offset[...] = result

    for d in range(1, n):
        o_copy(lax.rem(me + d, n)).wait_send()
    @pl.loop(0, tiles)
    def _(t):
        for d in range(1, h):
            p = lax.rem(chip + d, h)
            g_copy(p, t).wait_send()
            forward(p, t).wait_send()
        own_core_copy(t).wait_send()
        for st in range(2):
            for j in range(per_core):
                target, copy = part_copy(st, j, t)

                @pl.when(target != chip)
                def _():
                    copy.wait_send()


def shards(coeff, weight, upper_bound, lower_depth, slopes, state, adjoint):
    boxes, specs, width = coeff.shape
    n = lax.axis_size("neuron")
    h, rows = n // 2, boxes * specs
    per_core = h // 2
    total = width * n
    tile = min(width, 512)
    tiles = width // tile
    flat = lambda v: jnp.transpose(v, (1, 0, 2)).reshape(rows, width)
    dma = lambda *s: pltpu.SemaphoreType.DMA(s)
    vmem = pl.BlockSpec(memory_space=pltpu.VMEM)
    nc, offset, slope_grad, grad = pl.pallas_call(
        functools.partial(kernel, n, boxes, specs, tile, float(total) ** -0.5),
        out_shape=(
            jax.ShapeDtypeStruct((rows, width), BF16),
            jax.ShapeDtypeStruct((8, 128), F32),
            jax.ShapeDtypeStruct((boxes, width), F32),
            jax.ShapeDtypeStruct((rows, width), BF16),
        ),
        in_specs=[vmem] + [pl.BlockSpec(memory_space=pltpu.HBM)] * 5 + [vmem],
        out_specs=(vmem,) * 4,
        scratch_shapes=[
            pltpu.VMEM((boxes, width), F32),
            pltpu.VMEM((boxes, width), F32),
            pltpu.VMEM((boxes, width), F32),
            pltpu.VMEM((boxes, width), jnp.int32),
            pltpu.VMEM(weight.shape, BF16),
            pltpu.VMEM((rows, width), BF16),
            pltpu.VMEM((2, per_core, rows, width), F32),
            pltpu.VMEM((2, per_core, rows, width), F32),
            pltpu.VMEM((2, per_core, rows, width), F32),
            pltpu.VMEM((h, rows, width), F32),
            pltpu.VMEM((2 * boxes, width), BF16),
            pltpu.VMEM((2 * boxes, width), BF16),
            pltpu.VMEM((rows, width), BF16),
            pltpu.VMEM((n, rows, width), BF16),
            pltpu.VMEM((rows, width), BF16),
            pltpu.VMEM((rows, width), BF16),
            pltpu.VMEM((-(-boxes // 16) * 16, width), BF16),
            pltpu.VMEM((2, -(-boxes // 16) * 16, width), BF16),
            pltpu.VMEM((rows, width), F32),
            pltpu.VMEM((rows, width), BF16),
            pltpu.VMEM((rows, width), BF16),
            pltpu.VMEM((128, 128), F32),
            pltpu.VMEM((n, 8, 128), F32),
            dma(4), dma(h * tiles), dma(2), dma(2), dma(2),
            dma(2, per_core, tiles), dma(2, per_core, tiles), dma(2, per_core, tiles),
            dma(h, tiles), dma(h, tiles), dma(n, tiles), dma(h, tiles),
            dma(2), dma(2), dma(2), dma(tiles), dma(tiles), dma(n), dma(n),
        ],
        compiler_params=pltpu.CompilerParams(
            collective_id=0, has_side_effects=True, vmem_limit_bytes=48 * 1024 * 1024
        ),
        cost_estimate=pl.CostEstimate(
            flops=8 * rows * weight.size, bytes_accessed=2 * weight.size, transcendentals=0
        ),
    )(
        flat(coeff), weight, upper_bound, lower_depth, slopes, state, flat(adjoint),
    )
    wide = lambda v: jnp.transpose(v.reshape(specs, boxes, width), (1, 0, 2))
    return (
        wide(nc), jnp.transpose(offset[0, :rows].reshape(specs, boxes)), slope_grad, wide(grad),
    )


def solution(mesh):
    return jax.shard_map(
        shards,
        mesh=mesh,
        in_specs=(
            P("box", "spec", "neuron"),
            P("neuron", "spec"),
            P("box", "neuron"),
            P("box", "neuron"),
            P("box", "neuron"),
            P("box", "neuron"),
            P("box", "spec", "neuron"),
        ),
        out_specs=(
            P("box", "spec", "neuron"),
            P("box", "spec"),
            P("box", "neuron"),
            P("box", "spec", "neuron"),
        ),
        check_vma=False,
    )
```

profile of v0, /device:TPU:26, one launch (start us, length us, event | category | flops | bytes accessed | tf_op | source)
XLA Modules:
  0.0 69.0 jit_solution(10137292522224203658)
XLA Ops:
  0.6 1.2 %copy.11 = bf16[4,24,2048]{2,1,0:T(8,128)(2,1)S(1)} copy(bf16[4,24,2048]{2,0,1:T(4,128)(2,1)} %bitcast.15) | data formatting | bytes 786432 | tf_op jit(solution)/shard_map/transpose | solution.py:360
  1.8 1.2 %copy.12 = bf16[4,24,2048]{2,1,0:T(8,128)(2,1)S(1)} copy(bf16[4,24,2048]{2,0,1:T(4,128)(2,1)} %bitcast.16) | data formatting | bytes 786432 | tf_op jit(solution)/shard_map/transpose | solution.py:360
  3.1 0.0 copy-start
  3.1 0.9 %copy-done = f32[24,2048]{1,0:T(8,128)S(1)} copy-done((f32[24,2048]{1,0:T(8,128)S(1)}, f32[24,2048]{1,0:T(8,128)}, u32[]{:S(2)}) %copy-start) | copy-done | bytes 196632
  4.0 0.0 copy-start.1
  4.0 0.9 %copy-done.1 = f32[24,2048]{1,0:T(8,128)S(1)} copy-done((f32[24,2048]{1,0:T(8,128)S(1)}, f32[24,2048]{1,0:T(8,128)}, u32[]{:S(2)}) %copy-start.1) | copy-done | bytes 196632
  4.9 0.0 copy-start.2
  4.9 0.9 %copy-done.2 = f32[24,2048]{1,0:T(8,128)S(1)} copy-done((f32[24,2048]{1,0:T(8,128)S(1)}, f32[24,2048]{1,0:T(8,128)}, u32[]{:S(2)}) %copy-start.2) | copy-done | bytes 196632
  5.9 0.0 copy-start.3
  5.9 0.9 %copy-done.3 = s32[24,2048]{1,0:T(8,128)S(1)} copy-done((s32[24,2048]{1,0:T(8,128)S(1)}, s32[24,2048]{1,0:T(8,128)}, u32[]{:S(2)}) %copy-start.3) | copy-done | bytes 196632
  6.8 59.3 %shard_map.102 = (bf16[96,2048]{1,0:T(8,128)(2,1)S(1)}, f32[8,128]{1,0:T(8,128)S(1)}, f32[24,2048]{1,0:T(8,128)S(1)}, bf16[96,2048]{1,0:T(8,128)(2,1)S(1)}) custom-call(bf16[96,2048]{1,0:T(8,128)(2,1)S(1)} %bitcast.11, bf16[2048,4096]{1,0:T(8,128)(2,1)} %weight.1, f32[24,2048]{1,0:T(8,128)S(1)} %copy-done, f32[24,2048]{1,0:T(8,128)S(1)} %copy-done.1, ...), custom_call_target="tpu_custom_call" | custom-call | flops 6442450944 | bytes 16777216 | tf_op jit(solution)/shard_map/pallas_call | solution.py:363
  66.1 1.5 %copy_bitcast_fusion = (bf16[24,4,2048]{2,1,0:T(4,128)(2,1)}, bf16[24,4,2048]{2,1,0:T(4,128)(2,1)}) fusion(bf16[4,24,2048]{2,1,0:T(8,128)(2,1)S(1)} %bitcast.14, bf16[4,24,2048]{2,1,0:T(8,128)(2,1)S(1)} %bitcast.13), kind=kLoop, calls=%fused_computation | loop fusion | bytes 1572864 | tf_op jit(solution)/shard_map/transpose | solution.py:411
  67.6 0.7 reshape_squeeze.3
  68.3 0.7 copy.18
  (1 shorter events, 0.0 us)
Async XLA Ops:
  3.1 0.9 %copy-start = (f32[24,2048]{1,0:T(8,128)S(1)}, f32[24,2048]{1,0:T(8,128)}, u32[]{:S(2)}) copy-start(f32[24,2048]{1,0:T(8,128)} %upper_in.1) | copy-start | bytes 589828
  4.0 0.9 %copy-start.1 = (f32[24,2048]{1,0:T(8,128)S(1)}, f32[24,2048]{1,0:T(8,128)}, u32[]{:S(2)}) copy-start(f32[24,2048]{1,0:T(8,128)} %depth_in.1) | copy-start | bytes 589828
  4.9 0.9 %copy-start.2 = (f32[24,2048]{1,0:T(8,128)S(1)}, f32[24,2048]{1,0:T(8,128)}, u32[]{:S(2)}) copy-start(f32[24,2048]{1,0:T(8,128)} %slopes_in.1) | copy-start | bytes 589828
  5.9 0.9 %copy-start.3 = (s32[24,2048]{1,0:T(8,128)S(1)}, s32[24,2048]{1,0:T(8,128)}, u32[]{:S(2)}) copy-start(s32[24,2048]{1,0:T(8,128)} %state_in.1) | copy-start | bytes 589828
where the time goes:
time: 69.3 us; the launch traced here: 69 us
  Pallas kernels  59.3 us (86%)
  local copies, waits for them, and re-layouts  8.98 us (13%)
    pallas_call x1, Pallas kernels, shards(): pl.pallas_call(functools.partial(kernel, n, boxes, specs, tile, float(tot...  59.3 us
    unnamed x9, local copies, waits for them, and re-layouts  4.38 us
    transpose x2, local copies, waits for them, and re-layouts, shards(): flat = lambda v: jnp.transpose(v, (1, 0, 2)).reshape(rows, width)  2.44 us
    transpose x1, local copies, waits for them, and re-layouts, shards(): wide = lambda v: jnp.transpose(v.reshape(specs, boxes, width), (1, 0, 2))  1.48 us

commit v1 on v0

--- a/solution.py
+++ b/solution.py
@@ -16,9 +16,9 @@
     n, boxes, specs, tile, scale,
     coeff, weight, upper_in, depth_in, slopes_in, state_in, adjoint,
     new_coeff, offset, slope_grad, coeff_grad,
-    upper, depth, slopes, state, held, other, mine, theirs, crossed, parts, params, t_params, t_adjoint, cotan,
+    upper, depth, slopes, state, held, other, mine, theirs, crossed, coded, scales, parts, part_scales, params, t_params, t_adjoint, cotan,
     nc_out, nc_in, sg_out, sg_in, kept, away, back, off_part, offs,
-    i_sem, w_sem, a_sem, t_send, t_recv, c_send, c_recv, b_send, b_recv, g_send, g_recv, f_send,
+    i_sem, w_sem, a_sem, t_send, t_recv, c_send, c_recv, b_send, b_recv, d_send, d_recv, g_send, g_recv, f_send,
     n_sem, s_send, s_recv, e_send, e_recv, o_send, o_recv,
 ):
     me, sp = lax.axis_index("neuron"), lax.axis_index("spec")
@@ -106,9 +106,16 @@
         target = (1 - spec_half) * per_core + j
         cols = columns(0, t)
         return target, remote(
-            mine.at[st, j, :, cols], parts.at[chip, :, cols],
+            coded.at[st, j, :, cols], parts.at[chip, :, cols],
             b_send.at[st, j, t], b_recv.at[chip, t], target * 2 + core, sp,
-        )
+        ), remote(
+            scales.at[st, j, t], part_scales.at[chip, t],
+            d_send.at[st, j, t], d_recv.at[chip, t], target * 2 + core, sp,
+        )
+
+    diagonal = lax.broadcasted_iota(jnp.int32, (rows, 128), 0) == lax.broadcasted_iota(
+        jnp.int32, (rows, 128), 1
+    )
 
     for st in range(2):
         if st == 1:
@@ -135,15 +142,23 @@
                 rows_in[...], held[:, columns(2 * j + core, t)], preferred_element_type=F32
             )
             core_copy(st, j, t).wait()
-            mine[st, j, :, cols] = total + crossed[st, j, :, cols]
-            target, copy = part_copy(st, j, t)
+            total = total + crossed[st, j, :, cols]
+            target, copy, scale_copy = part_copy(st, j, t)
+
+            @pl.when(target == chip)
+            def _():
+                mine[:, cols] = total
 
             @pl.when(target != chip)
             def _():
+                largest = jnp.maximum(jnp.max(jnp.abs(total), axis=1, keepdims=True), 1e-30)
+                whole = jnp.round(total * (32766.0 / largest))
+                coded[st, j, :, cols] = whole.astype(jnp.int32).astype(jnp.int16)
+                step = jnp.where(diagonal, largest * (1.0 / 32766.0), 0.0)
+                scales[st, j, t] = jnp.broadcast_to(jnp.sum(step, axis=0, keepdims=True), (8, 128))
                 copy.start()
-
-    own_stage = jnp.where(half == sp, 0, 1)
-    own_j = lax.rem(chip, per_core)
+                scale_copy.start()
+
     adjoint_copy.wait()
     params_copy.wait()
 
@@ -164,15 +179,22 @@
     @pl.loop(0, tiles)
     def _(t):
         cols = columns(0, t)
-        pre = mine[own_stage, own_j, :, cols]
+        pre = mine[:, cols]
         for d in range(1, h):
             source = lax.rem(chip + d, h)
             pltpu.make_async_remote_copy(
-                src_ref=mine.at[0, 0, :, cols], dst_ref=parts.at[source, :, cols],
+                src_ref=coded.at[0, 0, :, cols], dst_ref=parts.at[source, :, cols],
                 send_sem=b_send.at[0, 0, t], recv_sem=b_recv.at[source, t],
                 device_id={"neuron": mate, "spec": sp}, device_id_type=MESH,
             ).wait_recv()
-            pre = pre + parts[source, :, cols]
+            pltpu.make_async_remote_copy(
+                src_ref=scales.at[0, 0, t], dst_ref=part_scales.at[source, t],
+                send_sem=d_send.at[0, 0, t], recv_sem=d_recv.at[source, t],
+                device_id={"neuron": mate, "spec": sp}, device_id_type=MESH,
+            ).wait_recv()
+            step = jnp.where(diagonal, part_scales[source, t][:1], 0.0)
+            step = jnp.sum(step, axis=1, keepdims=True)
+            pre = pre + parts[source, :, cols].astype(jnp.int32).astype(F32) * step
         both = t_params[:, cols].astype(F32)
         low = jnp.concatenate([both[:boxes]] * specs, axis=0)
         high = jnp.concatenate([both[boxes:]] * specs, axis=0)
@@ -285,12 +307,14 @@
         total = terms[:, :128]
         for c in range(1, tile // 128):
             total = total + terms[:, c * 128 : (c + 1) * 128]
-        off_part[:rows, :] += total
-
-    offs[me] = lax.dot_general(
-        jnp.ones((8, 128), F32), off_part[...], (((1,), (1,)), ((), ())),
-        precision=lax.Precision.HIGHEST, preferred_element_type=F32,
-    )
+        off_part[...] += total
+
+    lane = lax.broadcasted_iota(jnp.int32, (boxes, 128), 1)
+    result = jnp.zeros((boxes, 128), F32)
+    for k in range(specs):
+        one = jnp.sum(off_part[k * boxes : (k + 1) * boxes, :], axis=1, keepdims=True)
+        result = result + jnp.where(lane == k, one, 0.0)
+    offs[me] = result
 
     def o_copy(i):
         return remote(offs.at[me], offs.at[me], o_send.at[i], o_recv.at[me], i, sp)
@@ -329,7 +353,7 @@
     result = offs[0]
     for i in range(1, n):
         result = result + offs[i]
-    offset[...] = result
+    offset[...] = result[:, :specs]
 
     for d in range(1, n):
         o_copy(lax.rem(me + d, n)).wait_send()
@@ -342,11 +366,12 @@
         own_core_copy(t).wait_send()
         for st in range(2):
             for j in range(per_core):
-                target, copy = part_copy(st, j, t)
+                target, copy, scale_copy = part_copy(st, j, t)
 
                 @pl.when(target != chip)
                 def _():
                     copy.wait_send()
+                    scale_copy.wait_send()
 
 
 def shards(coeff, weight, upper_bound, lower_depth, slopes, state, adjoint):
@@ -364,7 +389,7 @@
         functools.partial(kernel, n, boxes, specs, tile, float(total) ** -0.5),
         out_shape=(
             jax.ShapeDtypeStruct((rows, width), BF16),
-            jax.ShapeDtypeStruct((8, 128), F32),
+            jax.ShapeDtypeStruct((boxes, specs), F32),
             jax.ShapeDtypeStruct((boxes, width), F32),
             jax.ShapeDtypeStruct((rows, width), BF16),
         ),
@@ -377,10 +402,13 @@
             pltpu.VMEM((boxes, width), jnp.int32),
             pltpu.VMEM(weight.shape, BF16),
             pltpu.VMEM((rows, width), BF16),
+            pltpu.VMEM((rows, width), F32),
             pltpu.VMEM((2, per_core, rows, width), F32),
             pltpu.VMEM((2, per_core, rows, width), F32),
-            pltpu.VMEM((2, per_core, rows, width), F32),
-            pltpu.VMEM((h, rows, width), F32),
+            pltpu.VMEM((2, per_core, rows, width), jnp.int16),
+            pltpu.VMEM((2, per_core, tiles, 8, 128), F32),
+            pltpu.VMEM((h, rows, width), jnp.int16),
+            pltpu.VMEM((h, tiles, 8, 128), F32),
             pltpu.VMEM((2 * boxes, width), BF16),
             pltpu.VMEM((2 * boxes, width), BF16),
             pltpu.VMEM((rows, width), BF16),
@@ -392,15 +420,15 @@
             pltpu.VMEM((rows, width), F32),
             pltpu.VMEM((rows, width), BF16),
             pltpu.VMEM((rows, width), BF16),
-            pltpu.VMEM((128, 128), F32),
-            pltpu.VMEM((n, 8, 128), F32),
+            pltpu.VMEM((rows, 128), F32),
+            pltpu.VMEM((n, boxes, 128), F32),
             dma(4), dma(h * tiles), dma(2), dma(2), dma(2),
             dma(2, per_core, tiles), dma(2, per_core, tiles), dma(2, per_core, tiles),
-            dma(h, tiles), dma(h, tiles), dma(n, tiles), dma(h, tiles),
+            dma(h, tiles), dma(2, per_core, tiles), dma(h, tiles), dma(h, tiles), dma(n, tiles), dma(h, tiles),
             dma(2), dma(2), dma(2), dma(tiles), dma(tiles), dma(n), dma(n),
         ],
         compiler_params=pltpu.CompilerParams(
-            collective_id=0, has_side_effects=True, vmem_limit_bytes=48 * 1024 * 1024
+            collective_id=0, has_side_effects=True, vmem_limit_bytes=63 * 1024 * 1024
         ),
         cost_estimate=pl.CostEstimate(
             flops=8 * rows * weight.size, bytes_accessed=2 * weight.size, transcendentals=0
@@ -410,7 +438,7 @@
     )
     wide = lambda v: jnp.transpose(v.reshape(specs, boxes, width), (1, 0, 2))
     return (
-        wide(nc), jnp.transpose(offset[0, :rows].reshape(specs, boxes)), slope_grad, wide(grad),
+        wide(nc), offset, slope_grad, wide(grad),
     )
 
 

time: 69.3 us -> 63.5 us (0.916)
  Pallas kernels: 59.3 us -> 52.6 us
    pallas_call x1, Pallas kernels: 59.3 us -> 52.6 us  [shards(): pl.pallas_call(functools.partial(kernel, n, boxes, specs, tile, float(tot...]
    transpose x2, local copies, waits for them, and re-layouts: 2.44 us -> 3.92 us  [shards(): flat = lambda v: jnp.transpose(v, (1, 0, 2)).reshape(rows, width)]
    unnamed x9 -> x2, local copies, waits for them, and re-layouts: 4.38 us -> 2.97 us
    transpose x1, local copies, waits for them, and re-layouts: 1.48 us -> 2.6 us  [shards(): wide = lambda v: jnp.transpose(v.reshape(specs, boxes, width), (1, 0, 2))]
where the time goes in v1:
time: 63.5 us; the launch traced here: 62.7 us
  Pallas kernels  52.6 us (83%)
  local copies, waits for them, and re-layouts  9.5 us (15%)
  between operations  0.64 us (1%)
    pallas_call x1, Pallas kernels, shards(): pl.pallas_call(functools.partial(kernel, n, boxes, specs, tile, float(tot...  52.6 us
    transpose x2, local copies, waits for them, and re-layouts, shards(): flat = lambda v: jnp.transpose(v, (1, 0, 2)).reshape(rows, width)  3.92 us
    unnamed x2, local copies, waits for them, and re-layouts  2.97 us
    transpose x1, local copies, waits for them, and re-layouts, shards(): wide = lambda v: jnp.transpose(v.reshape(specs, boxes, width), (1, 0, 2))  2.6 us

profile of v1, /device:TPU:26, one launch (start us, length us, event | category | flops | bytes accessed | tf_op | source)
XLA Modules:
  0.0 62.7 jit_solution(18054357574693176626)
XLA Ops:
  0.6 2.0 %copy.11 = bf16[4,24,2048]{2,1,0:T(8,128)(2,1)} copy(bf16[4,24,2048]{2,0,1:T(4,128)(2,1)} %bitcast.10) | data formatting | bytes 786432 | tf_op jit(solution)/shard_map/transpose | solution.py:385
  2.6 2.0 %copy.12 = bf16[4,24,2048]{2,1,0:T(8,128)(2,1)} copy(bf16[4,24,2048]{2,0,1:T(4,128)(2,1)} %bitcast.11) | data formatting | bytes 786432 | tf_op jit(solution)/shard_map/transpose | solution.py:385
  4.6 52.6 %shard_map.102 = (bf16[96,2048]{1,0:T(8,128)(2,1)}, f32[24,4]{1,0:T(8,128)}, f32[24,2048]{1,0:T(8,128)}, bf16[96,2048]{1,0:T(8,128)(2,1)}) custom-call(bf16[96,2048]{1,0:T(8,128)(2,1)} %bitcast.12, bf16[2048,4096]{1,0:T(8,128)(2,1)} %weight.1, f32[24,2048]{1,0:T(8,128)} %upper_in.1, f32[24,2048]{1,0:T(8,128)} %depth_in.1, f32[24,2048]{1,0:T(8,128)} %slopes_in.1, ...), custom_call_target="tpu_custom_call" | custom-call | flops 6442450944 | bytes 16777216 | tf_op jit(solution)/shard_map/pallas_call | solution.py:388
  57.1 2.6 %copy_bitcast_fusion = (bf16[24,4,2048]{2,1,0:T(4,128)(2,1)}, bf16[24,4,2048]{2,1,0:T(4,128)(2,1)}) fusion(bf16[4,24,2048]{2,1,0:T(8,128)(2,1)} %bitcast.15, bf16[4,24,2048]{2,1,0:T(8,128)(2,1)} %bitcast.14), kind=kLoop, calls=%fused_computation | loop fusion | bytes 1572864 | tf_op jit(solution)/shard_map/transpose | solution.py:439
  59.7 1.4 %copy.15 = f32[24,4]{0,1:T(4,128)} copy(f32[24,4]{1,0:T(8,128)} %get-tuple-element.13) | data formatting | bytes 768
  61.1 1.6 %copy.19 = f32[24,2048]{1,0:T(8,128)} copy(f32[24,2048]{1,0:T(8,128)} %get-tuple-element.24) | data formatting | bytes 393216

commit v2 on v1

v2 whole, which is shorter than its diff:
```python
import functools

import jax
import jax.numpy as jnp
from jax import lax
from jax.experimental import pallas as pl
from jax.experimental.pallas import tpu as pltpu
from jax.sharding import PartitionSpec as P

MESH = pl.DeviceIdType.MESH
F32 = jnp.float32
BF16 = jnp.bfloat16


def kernel(
    n, boxes, specs, tile, scale,
    coeff, weight, low, high, bound, adjoint,
    new_coeff, offset, slope_grad, coeff_grad,
    held, other, mine, theirs, crossed, coded, scales, parts, part_scales, t_adjoint, cotan,
    nc_out, nc_in, sg_sum, sg_out, sg_in, kept, away, back, off_part, offs,
    w_sem, a_sem, t_sem, c_send, c_recv, b_send, b_recv, d_send, d_recv, g_send, g_recv, f_send,
    n_sem, s_sem, e_send, e_recv, o_send, o_recv,
):
    me, sp = lax.axis_index("neuron"), lax.axis_index("spec")
    h = n // 2
    per_core = h // 2
    core, chip = lax.rem(me, 2), lax.div(me, 2)
    mate = me + 1 - 2 * core
    is_owner = lax.div(me, h) == sp
    not_owner = jnp.logical_not(is_owner)
    spot = lax.rem(me, h)
    rows, width = coeff.shape
    tiles = width // tile

    def remote(src, dst, send, recv, neuron, spec):
        return pltpu.make_async_remote_copy(
            src_ref=src, dst_ref=dst, send_sem=send, recv_sem=recv,
            device_id={"neuron": neuron, "spec": spec}, device_id_type=MESH,
        )

    def order(k):
        j = lax.rem(k, per_core)
        return 2 * j + jnp.where(k < per_core, 1 - core, core)

    def columns(q, t):
        return pl.ds(pl.multiple_of(q * width + t * tile, tile), tile)

    def load(k):
        q, t = order(lax.div(k, tiles)), lax.rem(k, tiles)
        return pltpu.make_async_copy(
            weight.at[:, columns(q, t)], held.at[:, columns(q, t)], w_sem.at[k]
        )

    @pl.loop(0, h * tiles)
    def _(k):
        load(k).start()

    barrier = pltpu.get_barrier_semaphore()
    for d in range(1, 2 * n):
        flat = lax.rem(me * 2 + sp + d, 2 * n)
        pl.semaphore_signal(
            barrier, inc=1,
            device_id={"neuron": lax.div(flat, 2), "spec": lax.rem(flat, 2)},
            device_id_type=MESH,
        )

    pl.semaphore_wait(barrier, 2 * n - 1)

    a_copy = remote(coeff, other, a_sem.at[0], a_sem.at[1], me, 1 - sp)
    a_copy.start()
    adjoint_copy = remote(adjoint, t_adjoint, t_sem.at[0], t_sem.at[1], me, 1 - sp)
    nc_copy = remote(nc_out, nc_in, n_sem.at[0], n_sem.at[1], me, 1 - sp)
    sg_copy = remote(sg_out, sg_in, s_sem.at[0], s_sem.at[1], me, 1 - sp)

    def core_copy(st, j, t):
        cols = columns(0, t)
        return remote(
            theirs.at[st, j, :, cols], crossed.at[st, j, :, cols],
            c_send.at[st, j, t], c_recv.at[st, j, t], mate, sp,
        )

    def part_copy(st, j, t):
        target = sp * per_core + j
        cols = columns(0, t)
        return target, remote(
            coded.at[st, j, :, cols], parts.at[st, chip, :, cols],
            b_send.at[st, j, t], b_recv.at[st, chip, t], target * 2 + core, sp,
        ), remote(
            scales.at[st, j, t], part_scales.at[st, chip, t],
            d_send.at[st, j, t], d_recv.at[st, chip, t], target * 2 + core, sp,
        )

    diagonal = lax.broadcasted_iota(jnp.int32, (rows, 128), 0) == lax.broadcasted_iota(
        jnp.int32, (rows, 128), 1
    )

    def block(st):
        return (sp if st == 0 else 1 - sp) * h + spot

    def g_copy(st, p, t):
        cols = columns(0, t)
        return remote(
            cotan.at[block(st), :, cols], cotan.at[block(st), :, cols],
            g_send.at[st, p, t], g_recv.at[block(st), t], p * 2 + core, sp,
        )

    def own_core_copy(st, t):
        cols = columns(0, t)
        return remote(
            cotan.at[block(st), :, cols], cotan.at[block(st), :, cols],
            g_send.at[st, chip, t], g_recv.at[block(st), t], mate, sp,
        )

    def relax(st):
        @pl.loop(0, tiles)
        def _(t):
            cols = columns(0, t)
            pre = mine[st, :, cols]
            for d in range(1, h):
                source = lax.rem(chip + d, h)
                pltpu.make_async_remote_copy(
                    src_ref=coded.at[0, 0, :, cols], dst_ref=parts.at[st, source, :, cols],
                    send_sem=b_send.at[0, 0, t], recv_sem=b_recv.at[st, source, t],
                    device_id={"neuron": mate, "spec": sp}, device_id_type=MESH,
                ).wait_recv()
                pltpu.make_async_remote_copy(
                    src_ref=scales.at[0, 0, t], dst_ref=part_scales.at[st, source, t],
                    send_sem=d_send.at[0, 0, t], recv_sem=d_recv.at[st, source, t],
                    device_id={"neuron": mate, "spec": sp}, device_id_type=MESH,
                ).wait_recv()
                step = jnp.where(diagonal, part_scales[st, source, t][:1], 0.0)
                step = jnp.sum(step, axis=1, keepdims=True)
                pre = pre + parts[st, source, :, cols].astype(jnp.int32).astype(F32) * step
            above = jnp.concatenate([low[:, cols]] * specs, axis=0)
            below = jnp.concatenate([high[:, cols]] * specs, axis=0)
            cot = (adjoint if st == 0 else t_adjoint)[:, cols].astype(F32)
            positive = jnp.maximum(pre, 0.0)
            cotan[block(st), :, cols] = (cot * jnp.where(pre > 0.0, above, below)).astype(BF16)
            for d in range(1, h):
                g_copy(st, lax.rem(chip + d, h), t).start()
            own_core_copy(st, t).start()
            relaxed = (above * positive + below * jnp.minimum(pre, 0.0)).astype(BF16)
            if st == 0:
                nc_in[:, cols] = relaxed
            else:
                nc_out[:, cols] = relaxed
            terms = cot * positive
            total = terms[:boxes]
            for s in range(1, specs):
                total = total + terms[s * boxes : (s + 1) * boxes]
            if st == 0:
                sg_sum[:, cols] = total
            else:
                total = jnp.where(bound[:, cols] > 0.0, total + sg_sum[:, cols], 0.0)
                slope_grad[:, cols] = total
                sg_out[:, cols] = jnp.concatenate(
                    [total, jnp.zeros((sg_out.shape[0] - boxes, tile), F32)], axis=0
                ).astype(BF16)

    for st in range(2):
        if st == 1:
            a_copy.wait()
        rows_in = coeff if st == 0 else other

        @pl.loop(0, per_core * tiles)
        def _(k):
            j, t = lax.div(k, tiles), lax.rem(k, tiles)
            if st == 0:
                load(k).wait()
            theirs[st, j, :, columns(0, t)] = jnp.dot(
                rows_in[...], held[:, columns(2 * j + 1 - core, t)], preferred_element_type=F32
            )
            core_copy(st, j, t).start()

        @pl.loop(0, per_core * tiles)
        def _(k):
            j, t = lax.div(k, tiles), lax.rem(k, tiles)
            cols = columns(0, t)
            if st == 0:
                load(k + per_core * tiles).wait()
            total = jnp.dot(
                rows_in[...], held[:, columns(2 * j + core, t)], preferred_element_type=F32
            )
            core_copy(st, j, t).wait()
            total = total + crossed[st, j, :, cols]
            target, copy, scale_copy = part_copy(st, j, t)

            @pl.when(target == chip)
            def _():
                mine[st, :, cols] = total

            @pl.when(target != chip)
            def _():
                largest = jnp.maximum(jnp.max(jnp.abs(total), axis=1, keepdims=True), 1e-30)
                whole = jnp.round(total * (32766.0 / largest))
                coded[st, j, :, cols] = whole.astype(jnp.int32).astype(jnp.int16)
                step = jnp.where(diagonal, largest * (1.0 / 32766.0), 0.0)
                scales[st, j, t] = jnp.broadcast_to(jnp.sum(step, axis=0, keepdims=True), (8, 128))
                copy.start()
                scale_copy.start()

        if st == 0:
            pl.when(not_owner)(adjoint_copy.start)
            pl.when(is_owner)(functools.partial(relax, 0))
        else:

            @pl.when(is_owner)
            def _():
                adjoint_copy.wait_recv()
                relax(1)
                nc_copy.start()
                sg_copy.start()

    def arrival(i, t):
        cols = columns(0, t)
        return pltpu.make_async_remote_copy(
            src_ref=cotan.at[i, :, cols], dst_ref=cotan.at[i, :, cols], send_sem=f_send.at[0, t],
            recv_sem=g_recv.at[i, t], device_id={"neuron": mate, "spec": sp},
            device_id_type=MESH,
        )

    def forward(i, t):
        cols = columns(0, t)
        return remote(
            cotan.at[i, :, cols], cotan.at[i, :, cols], f_send.at[i, t], g_recv.at[i, t], mate, sp
        )

    def e_copy(t):
        return remote(
            away.at[:, columns(0, t)], back.at[:, columns(0, t)], e_send.at[t], e_recv.at[t],
            me, 1 - sp,
        )

    def backward(spec_half):
        @pl.loop(0, tiles)
        def _(t):
            line = pl.ds(pl.multiple_of(t * tile, tile), tile)
            total = jnp.zeros((rows, tile), F32)
            for q in range(h):
                total = total + lax.dot_general(
                    cotan[spec_half * h + q], held[line, q * width : (q + 1) * width],
                    (((1,), (1,)), ((), ())), preferred_element_type=F32,
                )

            @pl.when(spec_half == sp)
            def _():
                kept[:, columns(0, t)] = total

            @pl.when(spec_half != sp)
            def _():
                away[:, columns(0, t)] = total.astype(BF16)
                e_copy(t).start()

    for spec_half in (sp, 1 - sp):
        for j in range(per_core):

            @pl.when(sp * per_core + j != chip)
            def _():
                @pl.loop(0, tiles)
                def _(t):
                    i = spec_half * h + 2 * j + core
                    arrival(i, t).wait_recv()
                    forward(i, t).start()

        @pl.loop(0, per_core * tiles)
        def _(k):
            i = spec_half * h + 2 * lax.div(k, tiles) + 1 - core
            arrival(i, lax.rem(k, tiles)).wait_recv()

        backward(spec_half)

    pl.when(not_owner)(nc_copy.wait_recv)
    off_part[...] = jnp.zeros_like(off_part)

    @pl.loop(0, tiles)
    def _(t):
        cols = columns(0, t)
        value = nc_in[:, cols]
        new_coeff[:, cols] = value
        depth = bound[:, cols] * scale
        terms = jnp.minimum(value.astype(F32), 0.0) * jnp.concatenate([depth] * specs, axis=0)
        total = terms[:, :128]
        for c in range(1, tile // 128):
            total = total + terms[:, c * 128 : (c + 1) * 128]
        off_part[...] += total

    lane = lax.broadcasted_iota(jnp.int32, (boxes, 128), 1)
    result = jnp.zeros((boxes, 128), F32)
    for k in range(specs):
        one = jnp.sum(off_part[k * boxes : (k + 1) * boxes, :], axis=1, keepdims=True)
        result = result + jnp.where(lane == k, one, 0.0)
    offs[me] = result

    def o_copy(i):
        return remote(offs.at[me], offs.at[me], o_send.at[i], o_recv.at[me], i, sp)

    for d in range(1, n):
        o_copy(lax.rem(me + d, n)).start()

    @pl.when(not_owner)
    def _():
        sg_copy.wait_recv()
        slope_grad[...] = sg_in[...].astype(F32)[:boxes]

    for t in range(tiles):
        e_copy(t).wait()
        cols = columns(0, t)
        coeff_grad[:, cols] = (kept[:, cols] + back[:, cols].astype(F32)).astype(BF16)

    for d in range(1, n):
        i = lax.rem(me + d, n)
        pltpu.make_async_remote_copy(
            src_ref=offs.at[i], dst_ref=offs.at[i], send_sem=o_send.at[me],
            recv_sem=o_recv.at[i], device_id={"neuron": mate, "spec": sp}, device_id_type=MESH,
        ).wait_recv()
    result = offs[0]
    for i in range(1, n):
        result = result + offs[i]
    offset[...] = result[:, :specs]

    for d in range(1, n):
        o_copy(lax.rem(me + d, n)).wait_send()
    @pl.when(is_owner)
    def _():
        nc_copy.wait_send()
        sg_copy.wait_send()

    pl.when(not_owner)(adjoint_copy.wait_send)

    @pl.loop(0, tiles)
    def _(t):
        @pl.when(is_owner)
        def _():
            for st in range(2):
                for d in range(1, h):
                    g_copy(st, lax.rem(chip + d, h), t).wait_send()
                own_core_copy(st, t).wait_send()

        for j in range(per_core):

            @pl.when(sp * per_core + j != chip)
            def _():
                for st in range(2):
                    _, copy, scale_copy = part_copy(st, j, t)
                    copy.wait_send()
                    scale_copy.wait_send()
                    forward(st * h + 2 * j + core, t).wait_send()


def shards(coeff, weight, upper_bound, lower_depth, slopes, state, adjoint):
    boxes, specs, width = coeff.shape
    n = lax.axis_size("neuron")
    h, rows = n // 2, boxes * specs
    per_core = h // 2
    total = width * n
    tile = min(width, 512)
    tiles = width // tile
    flat = lambda v: jnp.transpose(v, (1, 0, 2)).reshape(rows, width)
    dma = lambda *s: pltpu.SemaphoreType.DMA(s)
    vmem = pl.BlockSpec(memory_space=pltpu.VMEM)
    unstable = state == 2
    solid = jnp.where(state == 1, 1.0, 0.0)
    low = jnp.where(unstable, slopes, solid)
    high = jnp.where(unstable, upper_bound / (upper_bound + lower_depth), solid)
    bound = jnp.where(unstable, lower_depth, 0.0)
    nc, offset, slope_grad, grad = pl.pallas_call(
        functools.partial(kernel, n, boxes, specs, tile, float(total) ** -0.5),
        out_shape=(
            jax.ShapeDtypeStruct((rows, width), BF16),
            jax.ShapeDtypeStruct((boxes, specs), F32),
            jax.ShapeDtypeStruct((boxes, width), F32),
            jax.ShapeDtypeStruct((rows, width), BF16),
        ),
        in_specs=[vmem, pl.BlockSpec(memory_space=pltpu.HBM)] + [vmem] * 4,
        out_specs=(vmem,) * 4,
        scratch_shapes=[
            pltpu.VMEM(weight.shape, BF16),
            pltpu.VMEM((rows, width), BF16),
            pltpu.VMEM((2, rows, width), F32),
            pltpu.VMEM((2, per_core, rows, width), F32),
            pltpu.VMEM((2, per_core, rows, width), F32),
            pltpu.VMEM((2, per_core, rows, width), jnp.int16),
            pltpu.VMEM((2, per_core, tiles, 8, 128), F32),
            pltpu.VMEM((2, h, rows, width), jnp.int16),
            pltpu.VMEM((2, h, tiles, 8, 128), F32),
            pltpu.VMEM((rows, width), BF16),
            pltpu.VMEM((n, rows, width), BF16),
            pltpu.VMEM((rows, width), BF16),
            pltpu.VMEM((rows, width), BF16),
            pltpu.VMEM((boxes, width), F32),
            pltpu.VMEM((-(-boxes // 16) * 16, width), BF16),
            pltpu.VMEM((-(-boxes // 16) * 16, width), BF16),
            pltpu.VMEM((rows, width), F32),
            pltpu.VMEM((rows, width), BF16),
            pltpu.VMEM((rows, width), BF16),
            pltpu.VMEM((rows, 128), F32),
            pltpu.VMEM((n, boxes, 128), F32),
            dma(h * tiles), dma(2), dma(2),
            dma(2, per_core, tiles), dma(2, per_core, tiles), dma(2, per_core, tiles),
            dma(2, h, tiles), dma(2, per_core, tiles), dma(2, h, tiles),
            dma(2, h, tiles), dma(n, tiles), dma(n, tiles),
            dma(2), dma(2), dma(tiles), dma(tiles), dma(n), dma(n),
        ],
        compiler_params=pltpu.CompilerParams(
            collective_id=0, has_side_effects=True, vmem_limit_bytes=48 * 1024 * 1024
        ),
        cost_estimate=pl.CostEstimate(
            flops=8 * rows * weight.size, bytes_accessed=2 * weight.size, transcendentals=0
        ),
    )(
        flat(coeff), weight, low, high, bound, flat(adjoint),
    )
    wide = lambda v: jnp.transpose(v.reshape(specs, boxes, width), (1, 0, 2))
    return (
        wide(nc), offset, slope_grad, wide(grad),
    )


def solution(mesh):
    return jax.shard_map(
        shards,
        mesh=mesh,
        in_specs=(
            P("box", "spec", "neuron"),
            P("neuron", "spec"),
            P("box", "neuron"),
            P("box", "neuron"),
            P("box", "neuron"),
            P("box", "neuron"),
            P("box", "spec", "neuron"),
        ),
        out_specs=(
            P("box", "spec", "neuron"),
            P("box", "spec"),
            P("box", "neuron"),
            P("box", "spec", "neuron"),
        ),
        check_vma=False,
    )
```

time: 63.5 us -> 57.5 us (0.906)
  Pallas kernels: 52.6 us -> 48.1 us
  local copies, waits for them, and re-layouts: 9.5 us -> 5.25 us
  other arithmetic: 0 us -> 3.23 us
    pallas_call x1, Pallas kernels: 52.6 us -> 48.1 us  [shards(): pl.pallas_call(functools.partial(kernel, n, boxes, specs, tile, float(tot...]
    select_n x0 -> x3, other arithmetic: none -> 3.23 us  [the longest x1 1.2 us: shards(): high = jnp.where(unstable, upper_bound / (upper_bound + lower_depth), solid)]
    unnamed x2, local copies, waits for them, and re-layouts: 2.97 us -> 1.33 us
    transpose x2, local copies, waits for them, and re-layouts: 3.92 us -> 2.44 us  [shards(): flat = lambda v: jnp.transpose(v, (1, 0, 2)).reshape(rows, width)]
    transpose x1, local copies, waits for them, and re-layouts: 2.6 us -> 1.48 us  [shards(): wide = lambda v: jnp.transpose(v.reshape(specs, boxes, width), (1, 0, 2))]
where the time goes in v2:
time: 57.5 us; the launch traced here: 57.2 us
  Pallas kernels  48.1 us (84%)
  local copies, waits for them, and re-layouts  5.25 us (9%)
  other arithmetic  3.23 us (6%)
  between operations  0.65 us (1%)
    pallas_call x1, Pallas kernels, shards(): pl.pallas_call(functools.partial(kernel, n, boxes, specs, tile, float(tot...  48.1 us
    transpose x2, local copies, waits for them, and re-layouts, shards(): flat = lambda v: jnp.transpose(v, (1, 0, 2)).reshape(rows, width)  2.44 us
    transpose x1, local copies, waits for them, and re-layouts, shards(): wide = lambda v: jnp.transpose(v.reshape(specs, boxes, width), (1, 0, 2))  1.48 us
    unnamed x2, local copies, waits for them, and re-layouts  1.33 us
    select_n x1, other arithmetic, shards(): high = jnp.where(unstable, upper_bound / (upper_bound + lower_depth), solid)  1.2 us

profile of v2, /device:TPU:26, one launch (start us, length us, event | category | flops | bytes accessed | tf_op | source)
XLA Modules:
  0.0 57.2 jit_solution(11649602543531767886)
XLA Ops:
  0.6 1.1 %broadcast_select_fusion = (f32[24,2048]{1,0:T(8,128)S(1)}, pred[24,2048]{1,0:T(8,128)(4,1)S(1)}) fusion(f32[24,2048]{1,0:T(8,128)} %param.10, s32[24,2048]{1,0:T(8,128)} %param.12), kind=kLoop, calls=%fused_computation.5 | loop fusion | flops 98304 | bytes 638976 | tf_op jit(solution)/shard_map/jit(_where)/select_n | solution.py:365
  1.7 1.2 %select_select_fusion = (f32[24,2048]{1,0:T(8,128)S(1)}, pred[24,2048]{1,0:T(8,128)(4,1)S(1)}) fusion(pred[24,2048]{1,0:T(8,128)(4,1)S(1)} %get-tuple-element.17, f32[24,2048]{1,0:T(8,128)} %param.9, f32[24,2048]{1,0:T(8,128)} %param.10, s32[24,2048]{1,0:T(8,128)} %param.12), kind=kLoop, calls=%fused_computation.3 | loop fusion | flops 245760 | bytes 884736 | tf_op jit(solution)/shard_map/jit(_where)/select_n | solution.py:364
  2.9 1.0 %select_select_fusion.1.low = f32[24,2048]{1,0:T(8,128)S(1)} fusion(pred[24,2048]{1,0:T(8,128)(4,1)S(1)} %get-tuple-element.17, f32[24,2048]{1,0:T(8,128)} %param.11, pred[24,2048]{1,0:T(8,128)(4,1)S(1)} %get-tuple-element.19), kind=kLoop, calls=%fused_computation.4 | loop fusion | flops 98304 | bytes 491520 | tf_op jit(solution)/shard_map/jit(_where)/select_n | solution.py:363
  3.9 1.2 %copy.11 = bf16[4,24,2048]{2,1,0:T(8,128)(2,1)S(1)} copy(bf16[4,24,2048]{2,0,1:T(4,128)(2,1)} %bitcast.14) | data formatting | bytes 786432 | tf_op jit(solution)/shard_map/transpose | solution.py:358
  5.1 1.2 %copy.12 = bf16[4,24,2048]{2,1,0:T(8,128)(2,1)S(1)} copy(bf16[4,24,2048]{2,0,1:T(4,128)(2,1)} %bitcast.15) | data formatting | bytes 786432 | tf_op jit(solution)/shard_map/transpose | solution.py:358
  6.3 48.1 %shard_map.102 = (bf16[96,2048]{1,0:T(8,128)(2,1)S(1)}, f32[24,4]{1,0:T(8,128)S(1)}, f32[24,2048]{1,0:T(8,128)S(1)}, bf16[96,2048]{1,0:T(8,128)(2,1)S(1)}) custom-call(bf16[96,2048]{1,0:T(8,128)(2,1)S(1)} %bitcast.10, bf16[2048,4096]{1,0:T(8,128)(2,1)} %weight.1, f32[24,2048]{1,0:T(8,128)S(1)} %select_select_fusion.1.low, ...), custom_call_target="tpu_custom_call" | custom-call | flops 6442450944 | bytes 16777216 | tf_op jit(solution)/shard_map/pallas_call | solution.py:366
  54.4 1.5 %copy_bitcast_fusion = (bf16[24,4,2048]{2,1,0:T(4,128)(2,1)}, bf16[24,4,2048]{2,1,0:T(4,128)(2,1)}) fusion(bf16[4,24,2048]{2,1,0:T(8,128)(2,1)S(1)} %bitcast.13, bf16[4,24,2048]{2,1,0:T(8,128)(2,1)S(1)} %bitcast.12), kind=kLoop, calls=%fused_computation | loop fusion | bytes 1572864 | tf_op jit(solution)/shard_map/transpose | solution.py:413
  55.9 0.7 %copy.15 = f32[24,4]{0,1:T(4,128)} copy(f32[24,4]{1,0:T(8,128)S(1)} %get-tuple-element.13) | data formatting | bytes 768
  56.6 0.7 %copy.19 = f32[24,2048]{1,0:T(8,128)} copy(f32[24,2048]{1,0:T(8,128)S(1)} %get-tuple-element.28) | data formatting | bytes 393216

commit v3 on v2

--- a/solution.py
+++ b/solution.py
@@ -38,15 +38,13 @@
             device_id={"neuron": neuron, "spec": spec}, device_id_type=MESH,
         )
 
-    def order(k):
-        j = lax.rem(k, per_core)
-        return 2 * j + jnp.where(k < per_core, 1 - core, core)
-
     def columns(q, t):
         return pl.ds(pl.multiple_of(q * width + t * tile, tile), tile)
 
     def load(k):
-        q, t = order(lax.div(k, tiles)), lax.rem(k, tiles)
+        pair = lax.div(k, 2)
+        j, t = lax.div(pair, tiles), lax.rem(pair, tiles)
+        q = 2 * j + jnp.where(lax.rem(k, 2) == 0, 1 - core, core)
         return pltpu.make_async_copy(
             weight.at[:, columns(q, t)], held.at[:, columns(q, t)], w_sem.at[k]
         )
@@ -162,22 +160,20 @@
             a_copy.wait()
         rows_in = coeff if st == 0 else other
 
-        @pl.loop(0, per_core * tiles)
-        def _(k):
+        def give(k):
             j, t = lax.div(k, tiles), lax.rem(k, tiles)
             if st == 0:
-                load(k).wait()
+                load(2 * k).wait()
             theirs[st, j, :, columns(0, t)] = jnp.dot(
                 rows_in[...], held[:, columns(2 * j + 1 - core, t)], preferred_element_type=F32
             )
             core_copy(st, j, t).start()
 
-        @pl.loop(0, per_core * tiles)
-        def _(k):
+        def take(k):
             j, t = lax.div(k, tiles), lax.rem(k, tiles)
             cols = columns(0, t)
             if st == 0:
-                load(k + per_core * tiles).wait()
+                load(2 * k + 1).wait()
             total = jnp.dot(
                 rows_in[...], held[:, columns(2 * j + core, t)], preferred_element_type=F32
             )
@@ -198,6 +194,15 @@
                 scales[st, j, t] = jnp.broadcast_to(jnp.sum(step, axis=0, keepdims=True), (8, 128))
                 copy.start()
                 scale_copy.start()
+
+        give(0)
+
+        @pl.loop(1, per_core * tiles)
+        def _(k):
+            give(k)
+            take(k - 1)
+
+        take(per_core * tiles - 1)
 
         if st == 0:
             pl.when(not_owner)(adjoint_copy.start)

time: 57.5 us -> 58.1 us (1.010)
  Pallas kernels: 48.1 us -> 48.7 us
where the time goes in v3:
time: 58.1 us; the launch traced here: 57.8 us
  Pallas kernels  48.7 us (84%)
  local copies, waits for them, and re-layouts  5.25 us (9%)
  other arithmetic  3.23 us (6%)
  between operations  0.65 us (1%)
    pallas_call x1, Pallas kernels, shards(): pl.pallas_call(functools.partial(kernel, n, boxes, specs, tile, float(tot...  48.7 us
    transpose x2, local copies, waits for them, and re-layouts, shards(): flat = lambda v: jnp.transpose(v, (1, 0, 2)).reshape(rows, width)  2.44 us
    transpose x1, local copies, waits for them, and re-layouts, shards(): wide = lambda v: jnp.transpose(v.reshape(specs, boxes, width), (1, 0, 2))  1.48 us
    unnamed x2, local copies, waits for them, and re-layouts  1.33 us
    select_n x1, other arithmetic, shards(): high = jnp.where(unstable, upper_bound / (upper_bound + lower_depth), solid)  1.2 us

profile of v3, /device:TPU:26, one launch (start us, length us, event | category | flops | bytes accessed | tf_op | source)
XLA Modules:
  0.0 57.8 jit_solution(10452391338956343853)
XLA Ops:
  0.6 1.1 %broadcast_select_fusion = (f32[24,2048]{1,0:T(8,128)S(1)}, pred[24,2048]{1,0:T(8,128)(4,1)S(1)}) fusion(f32[24,2048]{1,0:T(8,128)} %param.10, s32[24,2048]{1,0:T(8,128)} %param.12), kind=kLoop, calls=%fused_computation.5 | loop fusion | flops 98304 | bytes 638976 | tf_op jit(solution)/shard_map/jit(_where)/select_n | solution.py:370
  1.7 1.2 %select_select_fusion = (f32[24,2048]{1,0:T(8,128)S(1)}, pred[24,2048]{1,0:T(8,128)(4,1)S(1)}) fusion(pred[24,2048]{1,0:T(8,128)(4,1)S(1)} %get-tuple-element.17, f32[24,2048]{1,0:T(8,128)} %param.9, f32[24,2048]{1,0:T(8,128)} %param.10, s32[24,2048]{1,0:T(8,128)} %param.12), kind=kLoop, calls=%fused_computation.3 | loop fusion | flops 245760 | bytes 884736 | tf_op jit(solution)/shard_map/jit(_where)/select_n | solution.py:369
  2.9 1.0 %select_select_fusion.1.low = f32[24,2048]{1,0:T(8,128)S(1)} fusion(pred[24,2048]{1,0:T(8,128)(4,1)S(1)} %get-tuple-element.17, f32[24,2048]{1,0:T(8,128)} %param.11, pred[24,2048]{1,0:T(8,128)(4,1)S(1)} %get-tuple-element.19), kind=kLoop, calls=%fused_computation.4 | loop fusion | flops 98304 | bytes 491520 | tf_op jit(solution)/shard_map/jit(_where)/select_n | solution.py:368
  3.9 1.2 %copy.11 = bf16[4,24,2048]{2,1,0:T(8,128)(2,1)S(1)} copy(bf16[4,24,2048]{2,0,1:T(4,128)(2,1)} %bitcast.14) | data formatting | bytes 786432 | tf_op jit(solution)/shard_map/transpose | solution.py:363
  5.1 1.2 %copy.12 = bf16[4,24,2048]{2,1,0:T(8,128)(2,1)S(1)} copy(bf16[4,24,2048]{2,0,1:T(4,128)(2,1)} %bitcast.15) | data formatting | bytes 786432 | tf_op jit(solution)/shard_map/transpose | solution.py:363
  6.3 48.7 %shard_map.102 = (bf16[96,2048]{1,0:T(8,128)(2,1)S(1)}, f32[24,4]{1,0:T(8,128)S(1)}, f32[24,2048]{1,0:T(8,128)S(1)}, bf16[96,2048]{1,0:T(8,128)(2,1)S(1)}) custom-call(bf16[96,2048]{1,0:T(8,128)(2,1)S(1)} %bitcast.10, bf16[2048,4096]{1,0:T(8,128)(2,1)} %weight.1, f32[24,2048]{1,0:T(8,128)S(1)} %select_select_fusion.1.low, ...), custom_call_target="tpu_custom_call" | custom-call | flops 6442450944 | bytes 16777216 | tf_op jit(solution)/shard_map/pallas_call | solution.py:371
  55.0 1.5 %copy_bitcast_fusion = (bf16[24,4,2048]{2,1,0:T(4,128)(2,1)}, bf16[24,4,2048]{2,1,0:T(4,128)(2,1)}) fusion(bf16[4,24,2048]{2,1,0:T(8,128)(2,1)S(1)} %bitcast.13, bf16[4,24,2048]{2,1,0:T(8,128)(2,1)S(1)} %bitcast.12), kind=kLoop, calls=%fused_computation | loop fusion | bytes 1572864 | tf_op jit(solution)/shard_map/transpose | solution.py:418
  56.5 0.7 %copy.15 = f32[24,4]{0,1:T(4,128)} copy(f32[24,4]{1,0:T(8,128)S(1)} %get-tuple-element.13) | data formatting | bytes 768
  57.1 0.7 %copy.19 = f32[24,2048]{1,0:T(8,128)} copy(f32[24,2048]{1,0:T(8,128)S(1)} %get-tuple-element.28) | data formatting | bytes 393216
